TPU v7x, 128 devices: a whole 4x4x4 slice. The times are simulated.
128 devices in a mesh: gx: 4 (over z), gy: 4 (over x_hi, core), gz: 8 (over x_lo, y).
Axes of the slice: x: 4 (x_hi: 2, x_lo: 2; x = x_hi * 2 + x_lo), y: 4, z: 4, core: 2. Of those that a mesh axis runs over, the one named last changes fastest.
Arguments:
- coords: float32 [3, 4, 4096, 128], P(None, 'gx', ('gy', 'gz')), may hold values from 0 to 11
- charges: float32 [4, 4096, 128], P('gx', ('gy', 'gz')), may hold values from -1.5 to 1.5
- atom_types: int32 [4, 4096, 128], P('gx', ('gy', 'gz')), may hold values from 0 to 63
- lj_sigma: float32 [64], replicated, may hold values from 2 to 4
- lj_epsilon: float32 [64], replicated, may hold values from 0.02 to 0.25
- tile_list: int32 [4, 4, 8, 2, 512], P('gx', 'gy', 'gz'), may hold values from -1 to 3455, as said below
Outputs:
- forces: float32 [3, 4, 4096, 128], P(None, 'gx', ('gy', 'gz'))
Inputs may be any that keep to these rules, and one draw needn't show every extreme that they name: tile_list[x, y, z, 0, t] is a block of brick (x, y, z) (0 to 127) and tile_list[x, y, z, 1, t] a block of its neighbourhood whose cell touches the home block's cell or is that cell (cell indices differ by at most one along each dimension, counted across brick faces periodically); on each brick the listed tiles come first and the remaining slots hold -1 in both rows; at least 256 tiles are listed on every brick and all 512 on some brick; tiles may repeat.
All inputs are finite; a program needn't handle non-finite values.
Results may differ from a plain program's by a relative error of at most 0.0003.
Values sent between devices are 32-bit elements; how exact they have to be, the bound alone decides.
No kernel may reach another device: no remote copies, remote signals or barrier semaphores. Data moves between devices by JAX's collectives and lax.ppermute only.
A program may use at most 128 MiB of HBM per device.

v0:
```python
import math

import jax
import jax.numpy as jnp
import numpy as np
from jax import lax
from jax.experimental import pallas as pl
from jax.experimental.pallas import tpu as pltpu
from jax.sharding import PartitionSpec as P

F32 = jnp.float32
BF16 = jnp.bfloat16

GRID = 4
LAYERS = 8
CELL = 11.0
LIMIT = 97.0
SCALE = LIMIT**-0.5
SOFT = 16.0 / LIMIT
COULOMB = 332.0636 / LIMIT
FACTOR_12 = 48.0 * LIMIT**-6.5
FACTOR_6 = 24.0 * LIMIT**-3.5

ROW_X, ROW_Y, ROW_Z, ROW_C, ROW_TYPE, ROW_Q, ROW_ONE, ROW_CC = range(8)
ROW_SOFT = ROW_TYPE
TYPES = 64
ORDER = 13
NX = 32
NY = 48
NZ = TYPES + 32
BATCH = 4
SIZES = (8, 4, 2, 1)
GROUP = 8
FAR_GROUP = 10
NEAR = 240
SENT = 56


def placements():
    home = np.zeros((32, NX), np.float32)
    src_w = np.zeros((NX, 32), np.float32)
    src_c = np.zeros((NX, 32), np.float32)
    at = 0

    def term(row, part):
        return part * 8 + row

    for row in (ROW_X, ROW_Y, ROW_Z):
        for i, j in ((0, 0), (0, 1), (1, 0), (1, 1), (0, 2), (2, 0)):
            home[term(row, i), at] = 1.0
            src_w[at, term(row, j)] = -2.0
            at += 1
    for part in range(3):
        home[term(ROW_SOFT, part), at] = 1.0
        src_w[at, term(ROW_ONE, 0)] = 1.0
        at += 1
    for part in range(3):
        home[term(ROW_ONE, 0), at] = 1.0
        src_w[at, term(ROW_Q, part)] = 1.0
        at += 1
    for i, j in ((0, 0), (0, 1), (1, 0), (1, 1), (0, 2), (2, 0)):
        home[term(ROW_CC, i), at] = 1.0
        src_c[at, term(ROW_C, j)] = 1.0
        at += 1
    place_r = np.zeros((16, 32), np.float32)
    for k, row in enumerate((ROW_X, ROW_Y, ROW_Z)):
        for part in range(3):
            place_r[4 * part + k, term(row, part)] = 1.0
    place_r[3, term(ROW_ONE, 0)] = 1.0
    return home, src_w, src_c, place_r


def weights(lj_sigma, lj_epsilon):
    root = jnp.sqrt(lj_epsilon)
    half = 0.5 * lj_sigma
    powers = [jnp.ones_like(half)]
    for _ in range(ORDER - 1):
        powers.append(powers[-1] * half)

    def halves(table):
        high = lax.reduce_precision(table, 8, 7)
        return high, table - high

    h_high, h_low = halves(jnp.stack([root * p for p in powers]))
    zero = jnp.zeros_like(half)
    p12 = jnp.stack([root * powers[12 - k] * (FACTOR_12 * math.comb(12, k)) for k in range(ORDER)])
    p6 = jnp.stack(
        [root * powers[6 - k] * (FACTOR_6 * math.comb(6, k)) if k <= 6 else zero for k in range(ORDER)]
    )
    pad = jnp.zeros((NY - 3 * ORDER, TYPES), F32)
    home_y = jnp.concatenate([h_high, h_high, h_low, pad])
    src_y = []
    for table in (p12, p6):
        high, low = halves(table)
        src_y += [high, low, high, pad]
    home_x, src_w, src_c, place_r = placements()
    home_x = np.pad(home_x, ((TYPES, 0), (0, 128 - NX)))
    home = jnp.concatenate([home_x, jnp.pad(home_y.T, ((0, NZ - TYPES), (0, 128 - NY)))], 1)
    fixed = jnp.concatenate([jnp.zeros((2 * NX + 16, TYPES)), np.concatenate([src_w, src_c, place_r])], 1)
    lj = jnp.concatenate([jnp.concatenate(src_y), jnp.zeros((2 * NY, 32), F32)], 1)
    source = jnp.concatenate([fixed, lj])
    return home.astype(BF16), source.astype(BF16)


def pack_kernel(half_hi, side, coords_in, charges_in, types_in, out, coords, charges, types, sems):
    copies = [
        pltpu.make_async_copy(source, target, sems.at[i])
        for i, (source, target) in enumerate(
            ((coords_in, coords), (charges_in, charges), (types_in, types))
        )
    ]
    for copy in copies:
        copy.start()
    for copy in copies:
        copy.wait()
    upper = half_hi[0] == 1
    back_y = side[0] == 3
    kinds = types[...].astype(F32)

    def next_y(value):
        ahead = jnp.concatenate([value[8:], value[:8]])
        behind = jnp.concatenate([value[24:], value[:24]])
        return jnp.where(back_y, behind, ahead)

    for q in range(5):
        for cell in range(5):

            def rows(k):
                if q < 3:
                    return coords[q, 32 * k : 32 * k + 32]
                return charges[32 * k : 32 * k + 32] if q == 3 else kinds[32 * k : 32 * k + 32]

            if cell < 4:
                value = rows(cell)
            else:
                ahead = pltpu.roll(rows(0).reshape(4, 8, 128), 7, 1)
                behind = pltpu.roll(rows(3).reshape(4, 8, 128), 1, 1)
                value = jnp.where(upper, behind, ahead).reshape(32, 128)
            out[pl.ds(5 * cell + q, 32, stride=SENT), :] = value
            out[pl.ds(25 + 5 * cell + q, 32, stride=SENT), :] = next_y(value)


def unpack_kernel(arrived, out):
    row = lax.broadcasted_iota(jnp.int32, (8, 128), 0)
    scale = jnp.where(row < 3, SCALE, 1.0)

    def body(cell_x, carry):
        off_x = (cell_x.astype(F32) - 2) * (CELL * SCALE)
        for s in range(8):
            cell_y, upper = s // 2, s % 2
            for c in range(10 if cell_y in (0, GRID - 1) else 5):
                place_y = cell_y + 1
                if c >= 5:
                    place_y = GRID + 1 if cell_y == 0 else 0
                place_z = upper * 4 + c % 5 + 1 if c % 5 < 4 else (1 - upper) * (LAYERS + 1)
                off_y = (place_y - 3) * (CELL * SCALE)
                off_z = (place_z - 5) * (CELL * SCALE)
                off = jnp.where(row == ROW_Y, off_y, jnp.where(row == ROW_Z, off_z, 0.0))
                off = jnp.where(row == ROW_X, off_x, off)
                rows = arrived[8 * cell_x + s, 5 * c : 5 * c + 5]
                block = jnp.concatenate([rows, jnp.zeros((3, 128), F32)]) * scale + off
                out[(cell_x * (GRID + 2) + place_y) * (LAYERS + 2) + place_z] = block
        return carry

    lax.fori_loop(0, GRID, body, 0)


def factors(block, off_x=None):
    row = lax.broadcasted_iota(jnp.int32, (8, 128), 0)
    kind = lax.broadcasted_iota(jnp.int32, (TYPES, 128), 0)
    moved = block if off_x is None else block + jnp.where(row == ROW_X, off_x, 0.0)
    square = jnp.sum(jnp.where(row < 3, moved * moved, 0.0), axis=0, keepdims=True)
    moved = jnp.where(row == ROW_Q, square, jnp.where(row == ROW_ONE, 1.0, moved))
    moved = jnp.where(row == ROW_SOFT, square + SOFT, moved)
    moved = jnp.where(row == ROW_CC, COULOMB * block[ROW_C : ROW_C + 1], moved)
    high = moved.astype(BF16).astype(F32)
    rest = moved - high
    mid = rest.astype(BF16).astype(F32)
    hot = jnp.where(block[ROW_TYPE : ROW_TYPE + 1].astype(jnp.int32) == kind, 1.0, 0.0)
    return jnp.concatenate([hot, high, mid, rest - mid, jnp.zeros((8, 128), F32)]).astype(BF16)


def store_source(places, z, w_src, rx, ry, rr):
    made = jnp.dot(w_src[...], z, preferred_element_type=F32).astype(BF16)
    for g, p in enumerate(places):
        own = made[:, 128 * g : 128 * g + 128]
        rx[p, :, :128] = own[:NX]
        rx[p, :, 128:] = own[NX : 2 * NX]
        rr[p, :, :128] = own[2 * NX : 2 * NX + 16]
        rr[p, :, 128:] = own[2 * NX : 2 * NX + 16]
        at = 2 * NX + 16
        ry[p, :, :128] = own[at : at + NY]
        ry[p, :, 128:] = own[at + NY :]


def store_home(first, z, w_home, lx, ly):
    made = lax.dot_general(z, w_home[...], (((0,), (0,)), ((), ())), preferred_element_type=F32)
    made = made.astype(BF16)
    for g in range(GROUP):
        own = made[128 * g : 128 * g + 128]
        lx[first + g] = own[:, :128]
        ly[first + g] = own[:, 128:]


def all_tiles(sizes, first, pairs, ids, lx, ly, rx, ry, rr, acc, buf_a, buf_b):
    def quantities(buf, batch, q):
        h, j = ids[0, batch * BATCH + q], ids[1, batch * BATCH + q]
        buf[q, 0] = jnp.dot(lx[h][:, :NX], rx[j], preferred_element_type=F32)
        buf[q, 1] = jnp.dot(ly[h][:, :NY], ry[j], preferred_element_type=F32)

    def forces(buf, batch, q):
        j, h = ids[1, batch * BATCH + q], ids[2, batch * BATCH + q]

        def part(i, side):
            return buf[q, i, :, 128 * side : 128 * side + 128].reshape(16, 8, 128)

        w = jnp.minimum(part(0, 0), 1.0)
        u, inv = lax.rsqrt(w), pltpu.reciprocal(w, approx=True)
        inv3 = inv * inv * inv
        c12, c6, charge = part(1, 0), part(1, 1), part(0, 1)
        push = inv * (inv3 * (inv3 * c12 - c6) + u * charge) - ((c12 - c6) + charge)
        push = push.reshape(128, 128)
        high = push.astype(BF16)
        low = (push - high.astype(F32)).astype(BF16)
        once = lax.dot_general(
            rr[j],
            jnp.concatenate([high, low], 1),
            (((1,), (1,)), ((), ())),
            preferred_element_type=F32,
        )
        acc[h] += once * ids[3, batch * BATCH + q].astype(F32)

    def both(buf_next, buf_now, batch_next, batch_now):
        for q in range(BATCH):
            quantities(buf_next, batch_next, q)
            forces(buf_now, batch_now, q)

    @pl.when(pairs > 0)
    def _():
        last = 2 * (first + pairs) - 1
        for q in range(BATCH):
            quantities(buf_a, 2 * first, q)

        def body(i, carry):
            both(buf_b, buf_a, 2 * i + 1, 2 * i)
            both(buf_a, buf_b, jnp.minimum(2 * i + 2, last), 2 * i + 1)
            return carry

        at = first
        for size in sizes:

            def several(i, carry, size=size, at=at):
                for k in range(size):
                    body(at + i * size + k, carry)
                return carry

            steps = (first + pairs - at) // size
            lax.fori_loop(0, steps, several, 0)
            at = at + steps * size


def near_place(b):
    return (b // (GRID * LAYERS) * (GRID + 2) + b // LAYERS % GRID + 1) * (LAYERS + 2) + b % LAYERS + 1


def near_kernel(steps, ids, region, w_home, w_src, acc, lx, ly, rx, ry, rr, buf_a, buf_b):
    def owned(i, carry):
        first = near_place(i * GROUP)
        places = [first + g for g in range(GROUP)]
        z = jnp.concatenate([factors(region[p]) for p in places], 1)
        store_source(places, z, w_src, rx, ry, rr)
        store_home(i * GROUP, z, w_home, lx, ly)
        return carry

    def rim_place(i):
        side, at = i // 28, i % 28
        place_y = jnp.where(at < 10, 0, jnp.where(at < 20, GRID + 1, 1 + (at - 20) // 2))
        place_z = jnp.where(at < 20, at % 10, (at - 20) % 2 * (LAYERS + 1))
        return (side * (GRID + 2) + place_y) * (LAYERS + 2) + place_z

    def rim(i, carry):
        places = [rim_place(i * GROUP + g) for g in range(GROUP)]
        z = jnp.concatenate([factors(region[p]) for p in places], 1)
        store_source(places, z, w_src, rx, ry, rr)
        return carry

    lax.fori_loop(0, 128 // GROUP, owned, 0, unroll=8)
    lax.fori_loop(0, 112 // GROUP, rim, 0, unroll=14)
    acc[...] = jnp.zeros_like(acc)
    all_tiles(SIZES, 0, steps[0], ids, lx, ly, rx, ry, rr, acc, buf_a, buf_b)


def far_kernel(steps, ids, low, high, region, w_src, lx, ly, acc, out, acc_out, rx, ry, rr, buf_a, buf_b):
    def prepare(i, carry):
        for k, (plane, off_x) in enumerate(((low, -44.0), (high, 44.0))):
            places = [i * FAR_GROUP + g for g in range(FAR_GROUP)]
            z = jnp.concatenate([factors(plane[p], off_x * SCALE) for p in places], 1)
            store_source([p + 60 * k for p in places], z, w_src, rx, ry, rr)
        return carry

    lax.fori_loop(0, 60 // FAR_GROUP, prepare, 0, unroll=6)
    all_tiles(SIZES, steps[0], steps[1], ids, lx, ly, rx, ry, rr, acc_out, buf_a, buf_b)

    def finish(s, carry):
        first = near_place(4 * s)
        for k in range(4):
            sums = acc_out[4 * s + k]
            head, tail = sums[:8], sums[8:]
            weighed = head + pltpu.roll(head, 4, 0) + tail
            out[s, 3 * k : 3 * k + 3] = (region[first + k] * head[3:4] - weighed)[:3]
        return carry

    lax.fori_loop(0, 32, finish, 0, unroll=8)


def tile_lists(tiles, blocks):
    home, source = tiles[0], tiles[1]
    slot, member = source // blocks, source % blocks
    step_x = slot // 9 - 1
    place_y = member // LAYERS % GRID + (slot // 3 % 3 - 1) * GRID + 1
    place_z = member % LAYERS + (slot % 3 - 1) * LAYERS + 1
    plane = place_y * (LAYERS + 2) + place_z
    side = jnp.where(step_x == 0, member // (GRID * LAYERS), (step_x + 1) // 2)
    listed = home >= 0
    unit = 2 * BATCH
    order = jnp.arange(home.shape[0])
    upto = order[None, :] <= order[:, None]
    key = home * (27 * blocks) + source
    same = key[None, :] == key[:, None]
    times = jnp.sum(jnp.where(same, 1, 0), 1)
    first = jnp.sum(jnp.where(same & upto, 1, 0), 1) == 1
    near = listed & first & (step_x == 0)
    far = listed & first & (step_x != 0)
    near_at = jnp.sum(jnp.where(upto & near[None, :], 1, 0), 1)
    far_at = jnp.sum(jnp.where(upto & far[None, :], 1, 0), 1)
    near_steps = (jnp.sum(near.astype(jnp.int32)) + unit - 1) // unit
    far_steps = (jnp.sum(far.astype(jnp.int32)) + unit - 1) // unit
    at = jnp.where(near, near_at - 1, jnp.where(far, near_steps * unit + far_at - 1, -1))
    code = home * 256 + side * 60 + plane + 1
    slots = jnp.arange(home.shape[0] + 2 * unit)
    found = jnp.sum(jnp.where(slots[:, None] == at[None, :], code[None, :], 0), 1)
    times = jnp.sum(jnp.where(slots[:, None] == at[None, :], times[None, :], 0), 1)
    real = found > 0
    code = jnp.maximum(found - 1, 0)
    ids = jnp.stack([code // 256, code % 256, jnp.where(real, code // 256, blocks), times])
    return jnp.stack([near_steps, far_steps]), ids


def per_device(coords, charges, atom_types, lj_sigma, lj_epsilon, tile_list):
    blocks, width = coords.shape[2], coords.shape[3]
    peers = lax.axis_size("gy") * lax.axis_size("gz")
    vmem = pl.BlockSpec(memory_space=pltpu.VMEM)
    smem = pl.BlockSpec(memory_space=pltpu.SMEM)
    gz = lax.axis_index("gz")
    small = pltpu.CompilerParams(vmem_limit_bytes=8 << 20)
    outgoing = pl.pallas_call(
        pack_kernel,
        out_shape=jax.ShapeDtypeStruct((peers * SENT, width), F32),
        in_specs=[smem, smem] + [pl.BlockSpec(memory_space=pl.ANY)] * 3,
        out_specs=vmem,
        scratch_shapes=[
            pltpu.VMEM((3, blocks, width), F32),
            pltpu.VMEM((blocks, width), F32),
            pltpu.VMEM((blocks, width), jnp.int32),
            pltpu.SemaphoreType.DMA((3,)),
        ],
        compiler_params=pltpu.CompilerParams(vmem_limit_bytes=65011712),
    )((gz % 2).reshape(1), (gz // 2).reshape(1), coords[:, 0], charges[0], atom_types[0])
    arrived = lax.all_to_all(
        outgoing.reshape(peers, SENT, width), ("gy", "gz"), split_axis=0, concat_axis=0, tiled=True
    )
    steps, ids = tile_lists(tile_list[0, 0, 0], blocks)
    w_home, w_src = weights(lj_sigma, lj_epsilon)
    region = pl.pallas_call(
        unpack_kernel,
        out_shape=jax.ShapeDtypeStruct((NEAR, 8, width), F32),
        in_specs=[vmem],
        out_specs=vmem,
        compiler_params=small,
    )(arrived)
    count = lax.axis_size("gx")
    forward = [(i, (i + 1) % count) for i in range(count)]
    backward = [(target, source) for source, target in forward]
    low = lax.ppermute(region[180:240], "gx", forward)
    high = lax.ppermute(region[:60], "gx", backward)

    def source_scratch(n):
        return [
            pltpu.VMEM((n, NX, 256), BF16),
            pltpu.VMEM((n, NY, 256), BF16),
            pltpu.VMEM((n, 16, 256), BF16),
            pltpu.VMEM((BATCH, 2, 128, 256), F32),
            pltpu.VMEM((BATCH, 2, 128, 256), F32),
        ]

    acc_shape = jax.ShapeDtypeStruct((blocks + 1, 16, width), F32)
    factor_shape = jax.ShapeDtypeStruct((blocks, 128, 128), BF16)
    acc, lx, ly = pl.pallas_call(
        near_kernel,
        out_shape=[acc_shape, factor_shape, factor_shape],
        in_specs=[smem, smem, vmem, vmem, vmem],
        out_specs=[vmem] * 3,
        scratch_shapes=source_scratch(NEAR),
        compiler_params=pltpu.CompilerParams(vmem_limit_bytes=28 << 20),
        cost_estimate=pl.CostEstimate(flops=10**10, bytes_accessed=10**7, transcendentals=10**6),
    )(steps, ids, region, w_home, w_src)
    totals, _ = pl.pallas_call(
        far_kernel,
        out_shape=[jax.ShapeDtypeStruct((peers, 12, width), F32), acc_shape],
        in_specs=[smem, smem] + [vmem] * 7,
        out_specs=[vmem] * 2,
        scratch_shapes=source_scratch(120),
        input_output_aliases={8: 1},
        compiler_params=pltpu.CompilerParams(vmem_limit_bytes=24 << 20),
    )(steps, ids, low, high, region, w_src, lx, ly, acc)
    back = lax.all_to_all(totals, ("gy", "gz"), split_axis=0, concat_axis=0, tiled=True)
    return back.reshape(peers, 4, 3, width).transpose(2, 1, 0, 3).reshape(3, 1, blocks, width)


def solution(mesh):
    return jax.shard_map(
        per_device,
        mesh=mesh,
        in_specs=(
            P(None, "gx", ("gy", "gz"), None),
            P("gx", ("gy", "gz"), None),
            P("gx", ("gy", "gz"), None),
            P(),
            P(),
            P("gx", "gy", "gz", None, None),
        ),
        out_specs=P(None, "gx", ("gy", "gz"), None),
        check_vma=False,
    )
```

profile of v0, /device:TPU:1, one launch (start us, length us, event | category | flops | bytes accessed | tf_op | source)
XLA Modules:
  0.0 76.2 jit_solution(6503096773717979474)
XLA Ops:
  0.0 2.0 %shard_map.82 = f32[1792,128]{1,0:T(8,128)} custom-call(s32[1]{0:T(128)} %bitcast.5.half_hi, s32[1]{0:T(128)} %bitcast.6.side, f32[3,128,128]{2,1,0:T(8,128)} %bitcast.83, f32[128,128]{1,0:T(8,128)} %bitcast.84, s32[128,128]{1,0:T(8,128)} %bitcast.85), custom_call_target="tpu_custom_call" | custom-call | tf_op jit(solution)/shard_map/pallas_call | solution.py:356
  2.0 0.0 copy-start.2
  2.1 0.0 copy-start.3
  2.1 0.0 copy-start.4
  2.1 0.0 copy-start.1
  2.1 0.0 copy-start
  2.1 8.7 %all-to-all-start = ((f32[32,56,128]{2,1,0:T(8,128)}), f32[32,56,128]{2,1,0:T(8,128)S(1)}, u32[]{:S(2)}, u32[]{:S(2)}) async-start(f32[32,56,128]{2,1,0:T(8,128)} %bitcast.81), calls=%async_computation | async-start | bytes 1835008 | tf_op jit(solution)/shard_map/all_to_all | solution.py:369
  10.9 0.0 copy-done.2
  10.9 0.4 fusion
  11.3 0.6 convert_reduce_fusion.1
  12.6 0.6 convert_reduce_fusion
  13.9 0.2 select_reduce_fusion.2
  14.2 0.4 select_reduce_fusion.1
  14.6 0.0 copy-done.3
  14.6 0.0 copy-done.4
  14.7 0.1 stack.174
  14.7 0.1 copy.70
  14.9 0.1 stack.160
  15.1 0.1 copy.69
  15.2 0.1 pad.15.clone
  15.3 0.7 concatenate.23
  16.0 0.1 pad_add_fusion.1.steps
  16.1 0.0 copy-done.1
  16.2 0.1 maximum_bitcast_fusion
  16.2 0.0 copy-done
  16.3 9.7 %all-to-all-done.arrived = f32[32,56,128]{2,1,0:T(8,128)S(1)} async-done(((f32[32,56,128]{2,1,0:T(8,128)}), f32[32,56,128]{2,1,0:T(8,128)S(1)}, u32[]{:S(2)}, u32[]{:S(2)}) %all-to-all-start) | async-done | bytes 917536 | tf_op jit(solution)/shard_map/all_to_all | solution.py:369
  26.0 0.2 shard_map.83.region
  26.2 3.8 %collective-permute-start.1 = (f32[60,8,128]{2,1,0:T(8,128)S(1)}, f32[60,8,128]{2,1,0:T(8,128)S(1)}, u32[]{:S(2)}, u32[]{:S(2)}) collective-permute-start(f32[60,8,128]{2,1,0:T(8,128)S(1)} %get-tuple-element.36), channel_id=1, source_target_pairs={{32,0},{64,32},{96,64},{0,96},{33,1},{65,33},{97,65},{1,97},{34,2}... | collective-permute-start | bytes 737288 | tf_op jit(solution)/shard_map/ppermute | solution.py:385
  30.0 0.0 collective-permute-start
  30.0 22.2 %shard_map.84 = (f32[129,16,128]{2,1,0:T(8,128)S(1)}, bf16[128,128,128]{2,1,0:T(8,128)(2,1)S(1)}, bf16[128,128,128]{2,1,0:T(8,128)(2,1)S(1)}) custom-call(s32[2]{0:T(128)S(1)} %pad_add_fusion.1.steps, s32[4,528]{1,0:T(4,128)S(1)} %pad_add_fusion.ids, f32[240,8,128]{2,1,0:T(8,128)S(1)} %shard_map.83.region, bf16[96,256]{1,0:T(8,128)(2,1)S(1)} %fusion.5.w_home, ...), custom_call_target="tpu_custom_call" | custom-call | flops 10000000000 | bytes 10000000 | tf_op jit(solution)/shard_map/pallas_call | solution.py:398
  52.2 0.0 collective-permute-done.1.high
  52.3 0.0 collective-permute-done.low
  52.3 5.8 %shard_map.85 = (f32[32,12,128]{2,1,0:T(8,128)S(1)}, f32[129,16,128]{2,1,0:T(8,128)S(1)}) custom-call(s32[2]{0:T(128)S(1)} %pad_add_fusion.1.steps, s32[4,528]{1,0:T(4,128)S(1)} %pad_add_fusion.ids, f32[60,8,128]{2,1,0:T(8,128)S(1)} %collective-permute-done.low, f32[60,8,128]{2,1,0:T(8,128)S(1)} %collective-permute-done.1.high, ...), custom_call_target="tpu_custom_call", output_to_operand_aliasing={{1}: (8, {})} | custom-call | tf_op jit(solution)/shard_map/pallas_call | solution.py:407
  58.1 17.3 %all_to_all.10 = f32[32,12,128]{2,1,0:T(8,128)S(1)} all-to-all(f32[32,12,128]{2,1,0:T(8,128)S(1)} %get-tuple-element.12), channel_id=1, replica_groups=mesh['gx'=4,'gy'=4,'gz'=8] {'gy','gz'}, dimensions={0} | all-to-all | bytes 393216 | tf_op jit(solution)/shard_map/all_to_all | solution.py:416
  75.4 0.1 copy.73
  75.5 0.7 copy.74
  (25 shorter events, 0.3 us)
Async XLA Ops:
  2.0 8.8 %copy-start.2 = (s32[1,1,1,2,512]{4,3,2,1,0:T(2,128)S(1)}, s32[1,1,1,2,512]{4,3,2,1,0:T(2,128)}, u32[]{:S(2)}) copy-start(s32[1,1,1,2,512]{4,3,2,1,0:T(2,128)} %param.13) | copy-start | bytes 12292
  2.1 12.5 %copy-start.3 = (f32[64]{0:T(128)S(1)}, f32[64]{0:T(128)}, u32[]{:S(2)}) copy-start(f32[64]{0:T(128)} %param.11) | copy-start | bytes 772
  2.1 12.5 %copy-start.4 = (f32[64]{0:T(128)S(1)}, f32[64]{0:T(128)}, u32[]{:S(2)}) copy-start(f32[64]{0:T(128)} %param.12) | copy-start | bytes 772
  2.1 14.0 %copy-start.1 = (bf16[80,96]{1,0:T(8,128)(2,1)S(1)}, bf16[80,96]{1,0:T(8,128)(2,1)}, u32[]{:S(2)}) copy-start(bf16[80,96]{1,0:T(8,128)(2,1)} %constant.242) | copy-start | bytes 46084
  2.1 14.1 %copy-start = (bf16[96,128]{1,0:T(8,128)(2,1)S(1)}, bf16[96,128]{1,0:T(8,128)(2,1)}, u32[]{:S(2)}) copy-start(bf16[96,128]{1,0:T(8,128)(2,1)} %constant.243) | copy-start | bytes 73732
  2.1 23.9 %all-to-all-start = ((f32[32,56,128]{2,1,0:T(8,128)}), f32[32,56,128]{2,1,0:T(8,128)S(1)}, u32[]{:S(2)}, u32[]{:S(2)}) async-start(f32[32,56,128]{2,1,0:T(8,128)} %bitcast.81), calls=%async_computation | async-start | bytes 1835008 | tf_op jit(solution)/shard_map/all_to_all | solution.py:369
  26.2 26.0 %collective-permute-start.1 = (f32[60,8,128]{2,1,0:T(8,128)S(1)}, f32[60,8,128]{2,1,0:T(8,128)S(1)}, u32[]{:S(2)}, u32[]{:S(2)}) collective-permute-start(f32[60,8,128]{2,1,0:T(8,128)S(1)} %get-tuple-element.36), channel_id=1, source_target_pairs={{32,0},{64,32},{96,64},{0,96},{33,1},{65,33},{97,65},{1,97},{34,2}... | collective-permute-start | bytes 737288 | tf_op jit(solution)/shard_map/ppermute | solution.py:385
  30.0 22.2 %collective-permute-start = (f32[60,8,128]{2,1,0:T(8,128)S(1)}, f32[60,8,128]{2,1,0:T(8,128)S(1)}, u32[]{:S(2)}, u32[]{:S(2)}) collective-permute-start(f32[60,8,128]{2,1,0:T(8,128)S(1)} %get-tuple-element.37), channel_id=1, source_target_pairs={{0,32},{32,64},{64,96},{96,0},{1,33},{33,65},{65,97},{97,1},{2,34}... | collective-permute-start | bytes 737288 | tf_op jit(solution)/shard_map/ppermute | solution.py:384
where the time goes:
time: 75.8 us; the launch traced here: 76.2 us
  Pallas kernels  30.3 us (40%)
  blocking collectives  17.3 us (23%)
  starting transfers between devices  12.6 us (17%)
  waiting for transfers between devices  9.71 us (13%)
  other arithmetic  2.65 us (3%)
  local copies, waits for them, and re-layouts  2.07 us (3%)
  between operations  1.61 us (2%)
    pallas_call x1, Pallas kernels, per_device(): pl.pallas_call(near_kernel, out_shape=[acc_shape, factor_shape, factor_sh...  22.2 us
    all_to_all x1, blocking collectives, per_device(): lax.all_to_all(totals, ('gy', 'gz'), split_axis=0, concat_axis=0, tiled=T...  17.3 us
    all_to_all x1, waiting for transfers between devices, per_device(): lax.all_to_all(outgoing.reshape(peers, SENT, width), ('gy', 'gz'), split_...  9.71 us
    all_to_all x1, starting transfers between devices, per_device(): lax.all_to_all(outgoing.reshape(peers, SENT, width), ('gy', 'gz'), split_...  8.74 us
    pallas_call x1, Pallas kernels, per_device(): pl.pallas_call(far_kernel, out_shape=[jax.ShapeDtypeStruct((peers, 12, wi...  5.83 us
    ppermute x1, starting transfers between devices, per_device(): high = lax.ppermute(region[:60], 'gx', backward)  3.83 us
    pallas_call x1, Pallas kernels, per_device(): pl.pallas_call(pack_kernel, out_shape=jax.ShapeDtypeStruct((peers * SENT,...  2.04 us
  transfers between devices with their start and end apart: 3, of which 1 were waited for; matrix products, arithmetic and copies ran while one was open for 5% of the time, Pallas kernels for 29%

commit v1 on v0

--- a/solution.py
+++ b/solution.py
@@ -215,7 +215,8 @@
             return buf[q, i, :, 128 * side : 128 * side + 128].reshape(16, 8, 128)
 
         w = jnp.minimum(part(0, 0), 1.0)
-        u, inv = lax.rsqrt(w), pltpu.reciprocal(w, approx=True)
+        u = lax.rsqrt(w)
+        inv = u * u
         inv3 = inv * inv * inv
         c12, c6, charge = part(1, 0), part(1, 1), part(0, 1)
         push = inv * (inv3 * (inv3 * c12 - c6) + u * charge) - ((c12 - c6) + charge)

time: 75.8 us -> 74.8 us (0.987); the launches traced: 76.2 us -> 74.4 us
  blocking collectives: 17.3 us -> 16.1 us
    all_to_all x1, blocking collectives: 17.3 us -> 16.1 us  [per_device(): lax.all_to_all(totals, ('gy', 'gz'), split_axis=0, concat_axis=0, tiled=T...]
    pallas_call x1, Pallas kernels: 22.2 us -> 21.1 us  [per_device(): pl.pallas_call(near_kernel, out_shape=[acc_shape, factor_shape, factor_sh...]
  transfers between devices with their start and end apart: 3 -> 3, of which waited for: 1 -> 1; matrix products, arithmetic and copies ran while one was open for 5% -> 5% of each run, Pallas kernels for 29% -> 28%
where the time goes in v1:
time: 74.8 us; the launch traced here: 74.4 us
  Pallas kernels  29.6 us (40%)
  blocking collectives  16.1 us (22%)
  starting transfers between devices  12.6 us (17%)
  waiting for transfers between devices  9.71 us (13%)
  other arithmetic  2.65 us (4%)
  local copies, waits for them, and re-layouts  2.07 us (3%)
  between operations  1.61 us (2%)
    pallas_call x1, Pallas kernels, per_device(): pl.pallas_call(near_kernel, out_shape=[acc_shape, factor_shape, factor_sh...  21.1 us
    all_to_all x1, blocking collectives, per_device(): lax.all_to_all(totals, ('gy', 'gz'), split_axis=0, concat_axis=0, tiled=T...  16.1 us
    all_to_all x1, waiting for transfers between devices, per_device(): lax.all_to_all(outgoing.reshape(peers, SENT, width), ('gy', 'gz'), split_...  9.71 us
    all_to_all x1, starting transfers between devices, per_device(): lax.all_to_all(outgoing.reshape(peers, SENT, width), ('gy', 'gz'), split_...  8.74 us
    pallas_call x1, Pallas kernels, per_device(): pl.pallas_call(far_kernel, out_shape=[jax.ShapeDtypeStruct((peers, 12, wi...  6.32 us
    ppermute x1, starting transfers between devices, per_device(): high = lax.ppermute(region[:60], 'gx', backward)  3.83 us
    pallas_call x1, Pallas kernels, per_device(): pl.pallas_call(pack_kernel, out_shape=jax.ShapeDtypeStruct((peers * SENT,...  2.04 us
  transfers between devices with their start and end apart: 3, of which 1 were waited for; matrix products, arithmetic and copies ran while one was open for 5% of the time, Pallas kernels for 28%

profile of v1, /device:TPU:1, one launch (start us, length us, event | category | flops | bytes accessed | tf_op | source)
XLA Modules:
  0.0 74.4 jit_solution(17775330982969767951)
XLA Ops:
  0.0 2.0 %shard_map.82 = f32[1792,128]{1,0:T(8,128)} custom-call(s32[1]{0:T(128)} %bitcast.5.half_hi, s32[1]{0:T(128)} %bitcast.6.side, f32[3,128,128]{2,1,0:T(8,128)} %bitcast.83, f32[128,128]{1,0:T(8,128)} %bitcast.84, s32[128,128]{1,0:T(8,128)} %bitcast.85), custom_call_target="tpu_custom_call" | custom-call | tf_op jit(solution)/shard_map/pallas_call | solution.py:357
  2.0 0.0 copy-start.2
  2.1 0.0 copy-start.3
  2.1 0.0 copy-start.4
  2.1 0.0 copy-start.1
  2.1 0.0 copy-start
  2.1 8.7 %all-to-all-start = ((f32[32,56,128]{2,1,0:T(8,128)}), f32[32,56,128]{2,1,0:T(8,128)S(1)}, u32[]{:S(2)}, u32[]{:S(2)}) async-start(f32[32,56,128]{2,1,0:T(8,128)} %bitcast.81), calls=%async_computation | async-start | bytes 1835008 | tf_op jit(solution)/shard_map/all_to_all | solution.py:370
  10.9 0.0 copy-done.2
  10.9 0.4 fusion
  11.3 0.6 convert_reduce_fusion.1
  12.6 0.6 convert_reduce_fusion
  13.9 0.2 select_reduce_fusion.2
  14.2 0.4 select_reduce_fusion.1
  14.6 0.0 copy-done.3
  14.6 0.0 copy-done.4
  14.7 0.1 stack.174
  14.7 0.1 copy.70
  14.9 0.1 stack.160
  15.1 0.1 copy.69
  15.2 0.1 pad.15.clone
  15.3 0.7 concatenate.23
  16.0 0.1 pad_add_fusion.1.steps
  16.1 0.0 copy-done.1
  16.2 0.1 maximum_bitcast_fusion
  16.2 0.0 copy-done
  16.3 9.7 %all-to-all-done.arrived = f32[32,56,128]{2,1,0:T(8,128)S(1)} async-done(((f32[32,56,128]{2,1,0:T(8,128)}), f32[32,56,128]{2,1,0:T(8,128)S(1)}, u32[]{:S(2)}, u32[]{:S(2)}) %all-to-all-start) | async-done | bytes 917536 | tf_op jit(solution)/shard_map/all_to_all | solution.py:370
  26.0 0.2 shard_map.83.region
  26.2 3.8 %collective-permute-start.1 = (f32[60,8,128]{2,1,0:T(8,128)S(1)}, f32[60,8,128]{2,1,0:T(8,128)S(1)}, u32[]{:S(2)}, u32[]{:S(2)}) collective-permute-start(f32[60,8,128]{2,1,0:T(8,128)S(1)} %get-tuple-element.36), channel_id=1, source_target_pairs={{32,0},{64,32},{96,64},{0,96},{33,1},{65,33},{97,65},{1,97},{34,2}... | collective-permute-start | bytes 737288 | tf_op jit(solution)/shard_map/ppermute | solution.py:386
  30.0 0.0 collective-permute-start
  30.0 21.1 %shard_map.84 = (f32[129,16,128]{2,1,0:T(8,128)S(1)}, bf16[128,128,128]{2,1,0:T(8,128)(2,1)S(1)}, bf16[128,128,128]{2,1,0:T(8,128)(2,1)S(1)}) custom-call(s32[2]{0:T(128)S(1)} %pad_add_fusion.1.steps, s32[4,528]{1,0:T(4,128)S(1)} %pad_add_fusion.ids, f32[240,8,128]{2,1,0:T(8,128)S(1)} %shard_map.83.region, bf16[96,256]{1,0:T(8,128)(2,1)S(1)} %fusion.5.w_home, ...), custom_call_target="tpu_custom_call" | custom-call | flops 10000000000 | bytes 10000000 | tf_op jit(solution)/shard_map/pallas_call | solution.py:399
  51.1 0.0 collective-permute-done.1.high
  51.1 0.0 collective-permute-done.low
  51.1 6.3 %shard_map.85 = (f32[32,12,128]{2,1,0:T(8,128)S(1)}, f32[129,16,128]{2,1,0:T(8,128)S(1)}) custom-call(s32[2]{0:T(128)S(1)} %pad_add_fusion.1.steps, s32[4,528]{1,0:T(4,128)S(1)} %pad_add_fusion.ids, f32[60,8,128]{2,1,0:T(8,128)S(1)} %collective-permute-done.low, f32[60,8,128]{2,1,0:T(8,128)S(1)} %collective-permute-done.1.high, ...), custom_call_target="tpu_custom_call", output_to_operand_aliasing={{1}: (8, {})} | custom-call | tf_op jit(solution)/shard_map/pallas_call | solution.py:408
  57.5 16.1 %all_to_all.10 = f32[32,12,128]{2,1,0:T(8,128)S(1)} all-to-all(f32[32,12,128]{2,1,0:T(8,128)S(1)} %get-tuple-element.12), channel_id=1, replica_groups=mesh['gx'=4,'gy'=4,'gz'=8] {'gy','gz'}, dimensions={0} | all-to-all | bytes 393216 | tf_op jit(solution)/shard_map/all_to_all | solution.py:417
  73.6 0.1 copy.73
  73.7 0.7 copy.74
  (25 shorter events, 0.3 us)
Async XLA Ops:
  2.0 8.8 %copy-start.2 = (s32[1,1,1,2,512]{4,3,2,1,0:T(2,128)S(1)}, s32[1,1,1,2,512]{4,3,2,1,0:T(2,128)}, u32[]{:S(2)}) copy-start(s32[1,1,1,2,512]{4,3,2,1,0:T(2,128)} %param.13) | copy-start | bytes 12292
  2.1 12.5 %copy-start.3 = (f32[64]{0:T(128)S(1)}, f32[64]{0:T(128)}, u32[]{:S(2)}) copy-start(f32[64]{0:T(128)} %param.11) | copy-start | bytes 772
  2.1 12.5 %copy-start.4 = (f32[64]{0:T(128)S(1)}, f32[64]{0:T(128)}, u32[]{:S(2)}) copy-start(f32[64]{0:T(128)} %param.12) | copy-start | bytes 772
  2.1 14.0 %copy-start.1 = (bf16[80,96]{1,0:T(8,128)(2,1)S(1)}, bf16[80,96]{1,0:T(8,128)(2,1)}, u32[]{:S(2)}) copy-start(bf16[80,96]{1,0:T(8,128)(2,1)} %constant.242) | copy-start | bytes 46084
  2.1 14.1 %copy-start = (bf16[96,128]{1,0:T(8,128)(2,1)S(1)}, bf16[96,128]{1,0:T(8,128)(2,1)}, u32[]{:S(2)}) copy-start(bf16[96,128]{1,0:T(8,128)(2,1)} %constant.243) | copy-start | bytes 73732
  2.1 23.9 %all-to-all-start = ((f32[32,56,128]{2,1,0:T(8,128)}), f32[32,56,128]{2,1,0:T(8,128)S(1)}, u32[]{:S(2)}, u32[]{:S(2)}) async-start(f32[32,56,128]{2,1,0:T(8,128)} %bitcast.81), calls=%async_computation | async-start | bytes 1835008 | tf_op jit(solution)/shard_map/all_to_all | solution.py:370
  26.2 24.9 %collective-permute-start.1 = (f32[60,8,128]{2,1,0:T(8,128)S(1)}, f32[60,8,128]{2,1,0:T(8,128)S(1)}, u32[]{:S(2)}, u32[]{:S(2)}) collective-permute-start(f32[60,8,128]{2,1,0:T(8,128)S(1)} %get-tuple-element.36), channel_id=1, source_target_pairs={{32,0},{64,32},{96,64},{0,96},{33,1},{65,33},{97,65},{1,97},{34,2}... | collective-permute-start | bytes 737288 | tf_op jit(solution)/shard_map/ppermute | solution.py:386
  30.0 21.1 %collective-permute-start = (f32[60,8,128]{2,1,0:T(8,128)S(1)}, f32[60,8,128]{2,1,0:T(8,128)S(1)}, u32[]{:S(2)}, u32[]{:S(2)}) collective-permute-start(f32[60,8,128]{2,1,0:T(8,128)S(1)} %get-tuple-element.37), channel_id=1, source_target_pairs={{0,32},{32,64},{64,96},{96,0},{1,33},{33,65},{65,97},{97,1},{2,34}... | collective-permute-start | bytes 737288 | tf_op jit(solution)/shard_map/ppermute | solution.py:385
